TPU v7x, 32 devices: a whole 2x2x4 slice. The times are simulated.
32 devices in a mesh: heads: 2 (over y), groups: 16 (over z, x, core).
Axes of the slice: x: 2, y: 2, z: 4, core: 2. Of those that a mesh axis runs over, the one named last changes fastest.
Arguments:
- hidden_rows: bfloat16 [192, 8192], P(None, 'groups'), may hold values from -6 to 6
- qkv_weight: bfloat16 [8192, 10240], P('groups', 'heads'), may hold values from -1 to 1
- out_weight: bfloat16 [8192, 8192], P('heads', 'groups'), may hold values from -0.0625 to 0.0625
- norm_gain: float32 [8192], P('groups'), may hold values from 0.5 to 1.5
- next_weight: bfloat16 [8192, 10240], P('groups', 'heads'), may hold values from -0.0625 to 0.0625
- cache_keys: bfloat16 [12288, 1024], P('groups', 'heads'), may hold values from -6 to 6
- cache_values: bfloat16 [12288, 1024], P('groups', 'heads'), may hold values from -6 to 6
- group_lengths: int32 [32], replicated, may hold values from 128 to 384, as said below
- group_owner: int32 [32], replicated, may hold values from 0 to 15, as said below
- group_start: int32 [32], replicated, may hold values from 0 to 8064, as said below
- listed_rows: int32 [192], replicated, may hold values from 0 to 8191, as said below
Outputs:
- hidden_out: bfloat16 [192, 8192], P(None, 'groups')
- next_qkv: bfloat16 [192, 10240], P('groups', 'heads')
Inputs may be any that keep to these rules, and one draw needn't show every extreme that they name: `group_lengths`: multiples of 128; groups 2k and 2k+1 together hold 512 tokens. `group_owner`: group 2k is held by owner k; every owner holds exactly two groups; one owner holds 768 tokens. The intervals from group_start to group_start + group_lengths - 1 of all groups tile 0 to 8191. `listed_rows`: distinct and increasing.
All inputs are finite; a program needn't handle non-finite values.
Results may differ from a plain program's by a relative error of at most 0.0085.
Values may be sent and summed in bfloat16 or wider, within the bound.
A program may use at most 128 MiB of HBM per device.

v0:
```python
import jax
import jax.numpy as jnp
from jax import lax
from jax.sharding import PartitionSpec as P

D = 8192
HD = 128
GQ = 8
BLK = 128


theta_base = 500000.0
epsilon = 1e-05
masked_score = -1e30


def angles(positions, half_dim):
    freq = theta_base ** (-(jnp.arange(half_dim).astype(jnp.float32) * 2.0 / (2 * half_dim)))
    phase = positions.astype(jnp.float32)[:, None] * freq[None, :]
    return (jnp.cos(phase), jnp.sin(phase))


def rotate(vectors, cosine, sine):
    half_dim = vectors.shape[-1] // 2
    lower = vectors[..., :half_dim]
    upper = vectors[..., half_dim:]
    return jnp.concatenate([lower * cosine - upper * sine, upper * cosine + lower * sine], axis=-1)


def layout(
    owner_index, group_lengths, group_owner, group_start, listed_rows, cap_blocks, block_rows
):
    block_len = group_lengths // block_rows
    holder = (group_owner == owner_index).astype(jnp.int32)
    held_blocks = holder * block_len
    offset = jnp.cumsum(held_blocks) - held_blocks
    block_ids = jnp.arange(cap_blocks)[:, None]
    member = (
        (holder[None, :] == 1)
        & (block_ids >= offset[None, :])
        & (block_ids < offset[None, :] + block_len[None, :])
    ).astype(jnp.int32)
    shift_blk = jnp.sum(member * group_start[None, :], axis=1)
    begin_blk = jnp.sum(
        member * (group_start[None, :] + (block_ids - offset[None, :]) * block_rows), axis=1
    )
    live_blk = jnp.sum(member, axis=1) > 0
    inside = jnp.arange(block_rows)[None, :]
    key_pos = (begin_blk[:, None] + inside).reshape(-1)
    key_shift = (shift_blk[:, None] + 0 * inside).reshape(-1)
    key_live = (live_blk[:, None] & (inside >= 0)).reshape(-1)
    listed_hit = jnp.any(key_pos[:, None] == listed_rows[None, :], axis=1)
    return (key_pos, key_shift, key_live & jnp.logical_not(listed_hit))


def on_device(
    hidden_rows,
    qkv_weight,
    out_weight,
    norm_gain,
    next_weight,
    cache_keys,
    cache_values,
    group_lengths,
    group_owner,
    group_start,
    listed_rows,
):
    group_count = lax.axis_size("groups")
    own_index = lax.axis_index("groups")
    row_count = hidden_rows.shape[0]
    local_rows = row_count // group_count
    kv_local = out_weight.shape[0] // (GQ * HD)
    capacity = cache_keys.shape[0]
    first_row = own_index * local_rows
    own_pos = lax.dynamic_slice_in_dim(listed_rows, first_row, local_rows)
    own_cos, own_sin = angles(own_pos, HD // 2)
    mixed = lax.psum_scatter(
        jnp.dot(hidden_rows, qkv_weight, preferred_element_type=jnp.float32),
        "groups",
        scatter_dimension=0,
        tiled=True,
    ).reshape(local_rows, kv_local, GQ + 2, HD)
    own_queries = rotate(mixed[:, :, :GQ], own_cos[:, None, None], own_sin[:, None, None]).astype(
        jnp.bfloat16
    )
    queries = lax.all_gather(own_queries, "groups", axis=0, tiled=True)
    own_keys = rotate(mixed[:, :, GQ], own_cos[:, None], own_sin[:, None]).astype(jnp.bfloat16)
    own_values = mixed[:, :, GQ + 1].astype(jnp.bfloat16)
    key_pos, key_shift, key_live = layout(
        own_index, group_lengths, group_owner, group_start, listed_rows, capacity // BLK, BLK
    )
    store_cos, store_sin = angles(key_shift, HD // 2)
    rotated = rotate(
        cache_keys.astype(jnp.float32).reshape(capacity, kv_local, HD),
        store_cos[:, None],
        store_sin[:, None],
    ).astype(jnp.bfloat16)
    store_values = cache_values.reshape(capacity, kv_local, HD)
    all_pos = jnp.concatenate([key_pos, own_pos], axis=0)
    all_live = jnp.concatenate([key_live, jnp.ones((local_rows,), bool)], axis=0)
    allowed = all_live[None, :] & (all_pos[None, :] <= listed_rows[:, None])
    scale = HD ** (-0.5)
    peak_list = []
    total_list = []
    numer_list = []
    for kv_head in range(kv_local):
        key_block = jnp.concatenate([rotated[:, kv_head], own_keys[:, kv_head]], axis=0)
        value_block = jnp.concatenate([store_values[:, kv_head], own_values[:, kv_head]], axis=0)
        for pair_index in range(GQ // 2):
            query_block = queries[:, kv_head, 2 * pair_index : 2 * pair_index + 2]
            scores = (
                jnp.einsum(
                    "rgd,kd->rgk", query_block, key_block, preferred_element_type=jnp.float32
                )
                * scale
            )
            scores = jnp.where(allowed[:, None, :], scores, masked_score)
            peaks = jnp.max(scores, axis=-1)
            weights = jnp.where(allowed[:, None, :], jnp.exp(scores - peaks[..., None]), 0.0)
            totals = jnp.sum(weights, axis=-1)
            numerator = jnp.einsum(
                "rgk,kd->rgd",
                weights.astype(jnp.bfloat16),
                value_block,
                preferred_element_type=jnp.float32,
            )
            peak_list.append(peaks)
            total_list.append(totals)
            numer_list.append(numerator)
    peaks = jnp.concatenate(peak_list, axis=1)
    totals = jnp.concatenate(total_list, axis=1)
    numerator = jnp.concatenate(numer_list, axis=1)
    highest = lax.pmax(peaks, "groups")
    factor = jnp.exp(peaks - highest)
    numerator, totals = lax.psum((numerator * factor[..., None], totals * factor), "groups")
    heads_out = (
        (numerator / totals[..., None]).astype(jnp.bfloat16).reshape(row_count, kv_local * GQ * HD)
    )
    head_term = jnp.dot(heads_out, out_weight, preferred_element_type=jnp.float32)
    attended = lax.psum(head_term.astype(jnp.bfloat16), "heads").astype(jnp.float32)
    resid = hidden_rows.astype(jnp.float32) + attended
    squares = lax.psum(jnp.sum(resid * resid, axis=1), "groups")
    normed = (resid * lax.rsqrt(squares / D + epsilon)[:, None] * norm_gain[None, :]).astype(
        jnp.bfloat16
    )
    next_qkv = lax.psum_scatter(
        jnp.dot(normed, next_weight, preferred_element_type=jnp.float32),
        "groups",
        scatter_dimension=0,
        tiled=True,
    ).astype(jnp.bfloat16)
    return (resid.astype(jnp.bfloat16), next_qkv)


def solution(mesh):
    in_specs = (
        P(None, "groups"),
        P("groups", "heads"),
        P("heads", "groups"),
        P("groups"),
        P("groups", "heads"),
        P("groups", "heads"),
        P("groups", "heads"),
        P(),
        P(),
        P(),
        P(),
    )
    out_specs = (P(None, "groups"), P("groups", "heads"))
    return jax.shard_map(
        on_device, mesh=mesh, in_specs=in_specs, out_specs=out_specs, check_vma=False
    )
```

profile of v0, /device:TPU:10, one launch (start us, length us, event | category | flops | bytes accessed | tf_op | source)
XLA Modules:
  0.0 526.6 jit_solution(15691661849498221785)
XLA Ops:
  7.2 5.7 %fusion.186 = f32[192,5120]{1,0:T(8,128)} fusion(bf16[192,512]{1,0:T(8,128)(2,1)} %param.11, bf16[512,5120]{1,0:T(8,128)(2,1)} %param.12), kind=kOutput, calls=%fused_computation.296 | convolution fusion | flops 1006632960 | bytes 9371648 | tf_op jit(solution)/shard_map/dot_general | solution.py:79
  12.9 61.5 %fusion = f32[16,5120]{1,0:T(8,128)S(1)} fusion(f32[192,5120]{1,0:T(8,128)} %fusion.186), kind=kCustom, calls=%all-reduce-scatter | all-reduce-scatter fusion | flops 1310721 | bytes 4260352
  74.4 3.1 collective-permute-start.2
  79.4 3.3 collective-permute-start
  83.5 3.5 collective-permute-start.3
  91.1 8.0 %collective-permute-done.3 = f32[12,5120]{1,0:T(8,128)} collective-permute-done((f32[12,5120]{1,0:T(8,128)}, f32[12,5120]{1,0:T(8,128)}, u32[]{:S(2)}, u32[]{:S(2)}) %collective-permute-start.3) | collective-permute-done | bytes 245792
  99.1 14.6 %concatenate.67 = f32[76,5120]{1,0:T(8,128)} concatenate(f32[12,5120]{1,0:T(8,128)} %collective-permute-done.3, f32[16,5120]{1,0:T(8,128)S(1)} %collective-permute-done.2, f32[16,5120]{1,0:T(8,128)} %collective-permute-done.1, f32[16,5120]{1,0:T(8,128)} %collective-permute-done, f32[16,5120]{1,0:T(8,128)S(1)} %fusion), dimensions={0} | concatenate | bytes 3112960
  131.6 27.8 %all-gather.2.cloned.1.call-done = bf16[192,4,8,128]{3,2,1,0:T(8,128)(2,1)} async-done(((bf16[12,4,8,128]{3,2,1,0:T(8,128)(2,1)}), bf16[192,4,8,128]{3,2,1,0:T(8,128)(2,1)}) %all-gather.2.cloned.1.call-update) | async-done | bytes 1572880 | tf_op jit(solution)/shard_map/all_gather | solution.py:87
  159.4 5.0 fusion.165
  189.2 49.1 %pmax.7 = f32[192,32]{0,1:T(8,128)} all-reduce(f32[192,32]{0,1:T(8,128)S(1)} %concatenate.65), channel_id=1, replica_groups=mesh['heads'=2,'groups'=16] {'groups'}, use_global_device_ids=true, to_apply=%region_22.23 | all-reduce | flops 6144 | bytes 49152 | tf_op jit(solution)/shard_map/pmax | solution.py:134
  247.7 3.2 fusion.55
  256.5 2.7 fusion.53
  261.5 2.2 broadcast_multiply_fusion
  263.8 59.5 %psum.29 = f32[192,32]{0,1:T(8,128)S(1)} all-reduce(f32[192,32]{0,1:T(8,128)S(1)} %get-tuple-element.21), channel_id=1, replica_groups=mesh['heads'=2,'groups'=16] {'groups'}, use_global_device_ids=true, to_apply=%region_40.41 | all-reduce | flops 6144 | bytes 49152 | tf_op jit(solution)/shard_map/psum | solution.py:136
  323.3 53.6 %all-reduce.8.cloned.1.call-done = f32[192,32,128]{2,0,1:T(8,128)} async-done(((f32[192,32,128]{2,0,1:T(8,128)}), f32[192,32,128]{2,0,1:T(8,128)}) %all-reduce.8.cloned.1.call-update) | async-done | bytes 3145744 | tf_op jit(solution)/shard_map/psum | solution.py:136
  376.9 4.9 fusion.22
  381.8 22.4 %all-reduce.10.cloned.1.call-done = bf16[192,512]{1,0:T(8,128)(2,1)} async-done(((bf16[192,512]{1,0:T(8,128)(2,1)}), bf16[192,512]{1,0:T(8,128)(2,1)}) %all-reduce.10.cloned.1.call-update) | async-done | bytes 196624 | tf_op jit(solution)/shard_map/psum | solution.py:141
  405.9 20.4 %psum.31 = f32[192]{0:T(256)S(1)} all-reduce(f32[192]{0:T(256)S(1)} %get-tuple-element.59), channel_id=1, replica_groups=mesh['heads'=2,'groups'=16] {'groups'}, use_global_device_ids=true, to_apply=%region_43.44 | all-reduce | flops 192 | bytes 1536 | tf_op jit(solution)/shard_map/psum | solution.py:143
  426.3 5.7 %fusion.122 = f32[192,5120]{1,0:T(8,128)} fusion(bf16[512,5120]{1,0:T(8,128)(2,1)} %param.15, bf16[192,512]{1,0:T(8,128)(2,1)} %all-reduce.10.cloned.1.call-done, bf16[192,512]{1,0:T(8,128)(2,1)S(1)} %copy-done, f32[512]{0:T(512)S(1)} %copy-done.26, f32[192]{0:T(256)S(1)} %add_rsqrt_fusion), kind=kOutput, calls=%fused_computation.176 | convolution fusion | flops 1007222784 | bytes 9571072 | tf_op jit(solution)/shard_map/dot_general | solution.py:148
  432.0 60.5 %fusion.1 = f32[16,5120]{1,0:T(8,128)S(1)} fusion(f32[192,5120]{1,0:T(8,128)} %fusion.122), kind=kCustom, calls=%all-reduce-scatter.1 | all-reduce-scatter fusion | flops 1310721 | bytes 4260352
  494.7 5.2 collective-permute-start.6
  499.9 3.3 collective-permute-start.4
  503.3 5.8 %collective-permute-start.7 = (bf16[12,5120]{1,0:T(8,128)(2,1)S(1)}, bf16[12,5120]{1,0:T(8,128)(2,1)S(1)}, u32[]{:S(2)}, u32[]{:S(2)}) collective-permute-start(bf16[12,5120]{1,0:T(8,128)(2,1)S(1)} %slice.209), channel_id=1, source_target_pairs={{0,4},{1,5},{2,6},{3,7},{4,8},{5,9},{6,10},{7,11},{8,12},{9,13},{1... | collective-permute-start | bytes 368648
  509.1 8.6 %collective-permute-done.7 = bf16[12,5120]{1,0:T(8,128)(2,1)S(1)} collective-permute-done((bf16[12,5120]{1,0:T(8,128)(2,1)S(1)}, bf16[12,5120]{1,0:T(8,128)(2,1)S(1)}, u32[]{:S(2)}, u32[]{:S(2)}) %collective-permute-start.7) | collective-permute-done | bytes 122912
  (235 shorter events, 71.7 us)
Async XLA Ops:
  7.2 152.2 %all-gather.2.cloned.1.call-start = ((), (), s32[]{:S(2)}) async-start(), calls=%async_computation | async-start | bytes 1671168 | tf_op jit(solution)/shard_map/all_gather | solution.py:87
  12.9 74.1 %copy-start.61 = (s32[32]{0:T(128)S(1)}, s32[32]{0:T(128)}, u32[]{:S(2)}) copy-start(s32[32]{0:T(128)} %param.19) | copy-start | bytes 388
  12.9 74.1 %copy-start.63 = (s32[32]{0:T(128)S(1)}, s32[32]{0:T(128)}, u32[]{:S(2)}) copy-start(s32[32]{0:T(128)} %param.18) | copy-start | bytes 388
  12.9 74.4 %copy-start.19 = (bf16[768,512]{1,0:T(8,128)(2,1)S(1)}, bf16[768,512]{1,0:T(8,128)(2,1)}, u32[]{:S(2)}) copy-start(bf16[768,512]{1,0:T(8,128)(2,1)} %param.16) | copy-start | bytes 2359300
  74.4 24.7 %collective-permute-start.2 = (f32[16,5120]{1,0:T(8,128)S(1)}, f32[16,5120]{1,0:T(8,128)S(1)}, u32[]{:S(2)}, u32[]{:S(2)}) collective-permute-start(f32[16,5120]{1,0:T(8,128)S(1)} %fusion), channel_id=1, source_target_pairs={{0,3},{1,4},{2,5},{3,6},{4,7},{5,8},{6,9},{7,10},{8,11},{9,12},{10... | collective-permute-start | bytes 983048
  77.5 21.6 %collective-permute-start.1 = (f32[16,5120]{1,0:T(8,128)S(1)}, f32[16,5120]{1,0:T(8,128)}, u32[]{:S(2)}, u32[]{:S(2)}) collective-permute-start(f32[16,5120]{1,0:T(8,128)S(1)} %fusion), channel_id=1, source_target_pairs={{0,2},{1,3},{2,4},{3,5},{4,6},{5,7},{6,8},{7,9},{8,10},{9,11},{10,... | collective-permute-start | bytes 983048
  79.4 19.6 %collective-permute-start = (f32[16,5120]{1,0:T(8,128)S(1)}, f32[16,5120]{1,0:T(8,128)}, u32[]{:S(2)}, u32[]{:S(2)}) collective-permute-start(f32[16,5120]{1,0:T(8,128)S(1)} %fusion), channel_id=1, source_target_pairs={{0,1},{1,2},{2,3},{3,4},{4,5},{5,6},{6,7},{7,8},{8,9},{9,10},{10,1... | collective-permute-start | bytes 983048
  83.5 15.6 %collective-permute-start.3 = (f32[12,5120]{1,0:T(8,128)}, f32[12,5120]{1,0:T(8,128)}, u32[]{:S(2)}, u32[]{:S(2)}) collective-permute-start(f32[12,5120]{1,0:T(8,128)} %slice.208), channel_id=1, source_target_pairs={{0,4},{1,5},{2,6},{3,7},{4,8},{5,9},{6,10},{7,11},{8,12},{9,13},{1... | collective-permute-start | bytes 737288
  115.7 261.2 %all-reduce.8.cloned.1.call-start = ((), (), s32[]{:S(2)}) async-start(), calls=%async_computation.1 | async-start | bytes 6291456 | tf_op jit(solution)/shard_map/psum | solution.py:136
  129.5 57.7 %copy-start.1 = (pred[192,780]{1,0:T(8,128)(4,1)}, pred[192,780]{1,0:T(8,128)(4,1)S(1)}, u32[]{:S(2)}) copy-start(pred[192,780]{1,0:T(8,128)(4,1)S(1)} %compare_and_fusion) | copy-start | bytes 449284
  168.9 20.1 %copy-start.27 = (f32[192,2]{0,1:T(2,128)}, f32[192,2]{0,1:T(2,128)S(1)}, u32[]{:S(2)}) copy-start(f32[192,2]{0,1:T(2,128)S(1)} %get-tuple-element.104) | copy-start | bytes 4612
  170.4 18.6 %copy-start.29 = (f32[192,2]{0,1:T(2,128)}, f32[192,2]{0,1:T(2,128)S(1)}, u32[]{:S(2)}) copy-start(f32[192,2]{0,1:T(2,128)S(1)} %get-tuple-element.102) | copy-start | bytes 4612
  171.9 17.1 %copy-start.31 = (f32[192,2]{0,1:T(2,128)}, f32[192,2]{0,1:T(2,128)S(1)}, u32[]{:S(2)}) copy-start(f32[192,2]{0,1:T(2,128)S(1)} %get-tuple-element.94) | copy-start | bytes 4612
  187.3 51.1 %copy-start.51 = (f32[192,2]{0,1:T(2,128)}, f32[192,2]{0,1:T(2,128)S(1)}, u32[]{:S(2)}) copy-start(f32[192,2]{0,1:T(2,128)S(1)} %get-tuple-element.90) | copy-start | bytes 4612
  187.3 51.1 %copy-start.24 = (bf16[768,1,128]{2,0,1:T(8,128)(2,1)S(1)}, bf16[768,1,128]{2,0,1:T(8,128)(2,1)}, u32[]{:S(2)}) copy-start(bf16[768,1,128]{2,0,1:T(8,128)(2,1)} %copy.152) | copy-start | bytes 589828
  189.0 49.4 %copy-start.53 = (f32[192,2]{0,1:T(2,128)}, f32[192,2]{0,1:T(2,128)S(1)}, u32[]{:S(2)}) copy-start(f32[192,2]{0,1:T(2,128)S(1)} %get-tuple-element.92) | copy-start | bytes 4612
  189.0 51.3 %copy-start.2 = (pred[192,780]{1,0:T(8,128)(4,1)S(1)}, pred[192,780]{1,0:T(8,128)(4,1)}, u32[]{:S(2)}) copy-start(pred[192,780]{1,0:T(8,128)(4,1)} %copy-done.1) | copy-start | bytes 449284
  263.7 140.5 %all-reduce.10.cloned.1.call-start = ((), (), s32[]{:S(2)}) async-start(), calls=%async_computation.2 | async-start | bytes 393216 | tf_op jit(solution)/shard_map/psum | solution.py:141
  323.3 81.0 %copy-start = (bf16[192,512]{1,0:T(8,128)(2,1)S(1)}, bf16[192,512]{1,0:T(8,128)(2,1)}, u32[]{:S(2)}) copy-start(bf16[192,512]{1,0:T(8,128)(2,1)} %param.11) | copy-start | bytes 589828
  323.3 103.0 %copy-start.26 = (f32[512]{0:T(512)S(1)}, f32[512]{0:T(512)}, u32[]{:S(2)}) copy-start(f32[512]{0:T(512)} %param.14) | copy-start | bytes 6148
  492.6 25.1 %collective-permute-start.5 = (bf16[16,5120]{1,0:T(8,128)(2,1)S(1)}, bf16[16,5120]{1,0:T(8,128)(2,1)S(1)}, u32[]{:S(2)}, u32[]{:S(2)}) collective-permute-start(bf16[16,5120]{1,0:T(8,128)(2,1)S(1)} %convert.46), channel_id=1, source_target_pairs={{0,2},{1,3},{2,4},{3,5},{4,6},{5,7},{6,8},{7,9},{8,10},{9,11},{10,... | collective-permute-start | bytes 491528
  494.7 23.0 %collective-permute-start.6 = (bf16[16,5120]{1,0:T(8,128)(2,1)S(1)}, bf16[16,5120]{1,0:T(8,128)(2,1)S(1)}, u32[]{:S(2)}, u32[]{:S(2)}) collective-permute-start(bf16[16,5120]{1,0:T(8,128)(2,1)S(1)} %convert.46), channel_id=1, source_target_pairs={{0,3},{1,4},{2,5},{3,6},{4,7},{5,8},{6,9},{7,10},{8,11},{9,12},{10... | collective-permute-start | bytes 491528
  499.9 17.8 %collective-permute-start.4 = (bf16[16,5120]{1,0:T(8,128)(2,1)S(1)}, bf16[16,5120]{1,0:T(8,128)(2,1)S(1)}, u32[]{:S(2)}, u32[]{:S(2)}) collective-permute-start(bf16[16,5120]{1,0:T(8,128)(2,1)S(1)} %convert.46), channel_id=1, source_target_pairs={{0,1},{1,2},{2,3},{3,4},{4,5},{5,6},{6,7},{7,8},{8,9},{9,10},{10,1... | collective-permute-start | bytes 491528
  503.3 14.4 %collective-permute-start.7 = (bf16[12,5120]{1,0:T(8,128)(2,1)S(1)}, bf16[12,5120]{1,0:T(8,128)(2,1)S(1)}, u32[]{:S(2)}, u32[]{:S(2)}) collective-permute-start(bf16[12,5120]{1,0:T(8,128)(2,1)S(1)} %slice.209), channel_id=1, source_target_pairs={{0,4},{1,5},{2,6},{3,7},{4,8},{5,9},{6,10},{7,11},{8,12},{9,13},{1... | collective-permute-start | bytes 368648
  (53 other events, 156.9 us)
Sparse Core Ops, SparseCore 0:
  115.8 43.5 all-gather.1
  263.9 113.0 all-reduce.7
  382.0 22.2 all-reduce.9
where the time goes:
time: 529 us; the launch traced here: 527 us
  blocking collectives  251 us (47%)
  waiting for transfers between devices  121 us (23%)
  matrix products  51.8 us (10%)
  local copies, waits for them, and re-layouts  40.3 us (8%)
  starting transfers between devices  28.5 us (5%)
  other arithmetic  19.1 us (4%)
  between operations  15.4 us (3%)
    unnamed x2, blocking collectives  122 us
    psum x1, blocking collectives, on_device(): lax.psum((numerator * factor[..., None], totals * factor), 'groups')  59.5 us
    psum x1, waiting for transfers between devices, on_device(): lax.psum((numerator * factor[..., None], totals * factor), 'groups')  53.6 us
    pmax x1, blocking collectives, on_device(): highest = lax.pmax(peaks, 'groups')  49.1 us
    unnamed x151, local copies, waits for them, and re-layouts  32.4 us
    unnamed x8, starting transfers between devices  28.2 us
    all_gather x1, waiting for transfers between devices, on_device(): queries = lax.all_gather(own_queries, 'groups', axis=0, tiled=True)  27.8 us
    dot_general x16, matrix products, on_device(): jnp.einsum('rgd,kd->rgk', query_block, key_block, preferred_element_type=...  24.6 us
  transfers between devices with their start and end apart: 11, of which 5 were waited for; matrix products, arithmetic and copies ran while one was open for 4% of the time, Pallas kernels for 0%

commit v1 on v0

v1 whole, which is shorter than its diff:
```python
import functools

import jax
import jax.numpy as jnp
from jax import lax
from jax.experimental import pallas as pl
from jax.experimental.pallas import tpu as pltpu
from jax.sharding import PartitionSpec as P

HD = 128
GQ = 8
BLK = 128
MESH = pl.DeviceIdType.MESH
theta_base = 500000.0
epsilon = 1e-05
masked_score = -1e30
NEVER = 1 << 30
LIMIT = 56 * 1024 * 1024


def angles(positions, half_dim):
    freq = theta_base ** (-(jnp.arange(half_dim).astype(jnp.float32) * 2.0 / (2 * half_dim)))
    phase = positions.astype(jnp.float32)[:, None] * freq[None, :]
    return (jnp.cos(phase), jnp.sin(phase))


def full_angles(positions):
    cosine, sine = angles(positions, HD // 2)
    return (
        jnp.concatenate([cosine, cosine], axis=1),
        jnp.concatenate([-sine, sine], axis=1),
    )


def round_up(value, unit):
    return (value + unit - 1) // unit * unit


def remote(src, dst, send_sem, recv_sem, axis, index):
    return pltpu.make_async_remote_copy(
        src_ref=src,
        dst_ref=dst,
        send_sem=send_sem,
        recv_sem=recv_sem,
        device_id={axis: index},
        device_id_type=MESH,
    )


def sibling_of(me):
    return me + 1 - 2 * (me % 2)


def across_of(me):
    return me + 2 - 4 * ((me // 2) % 2)


def greet_pairs(count):
    me = lax.axis_index("groups")
    chips = count // 2
    barrier = pltpu.get_barrier_semaphore()
    pl.semaphore_signal(
        barrier, inc=1, device_id={"groups": sibling_of(me)}, device_id_type=MESH
    )

    @pl.loop(1, chips)
    def _(k):
        other = ((me // 2 + k) % chips) * 2 + me % 2
        pl.semaphore_signal(barrier, inc=1, device_id={"groups": other}, device_id_type=MESH)

    pl.semaphore_wait(barrier, chips)


def gather_chunks(count, out, sems):
    send_a, recv_a, send_b, recv_b, send_c, recv_c = sems
    me = lax.axis_index("groups")
    rows = count // 4
    mine = me // 4
    lane = me % 4
    lane_across = across_of(me) % 4
    lane_sibling = sibling_of(me) % 4
    lane_diagonal = 3 - lane

    def along(k):
        place = (mine + k) % rows
        return remote(
            out.at[me], out.at[me], send_a.at[k], recv_a.at[mine], "groups", place * 4 + lane
        )

    def along_in(k):
        place = (mine + k) % rows
        slot = place * 4 + lane
        return remote(out.at[slot], out.at[slot], send_a.at[k], recv_a.at[place], "groups", slot)

    def across(place, at_lane):
        slot = place * 4 + at_lane
        return remote(
            out.at[slot],
            out.at[slot],
            send_b.at[place],
            recv_b.at[place],
            "groups",
            across_of(me),
        )

    def sideways(place, at_lane, half):
        slot = place * 4 + at_lane
        return remote(
            out.at[slot],
            out.at[slot],
            send_c.at[half, place],
            recv_c.at[half, place],
            "groups",
            sibling_of(me),
        )

    @pl.loop(1, rows)
    def _(k):
        along(k).start()

    across(mine, lane).start()
    sideways(mine, lane, 0).start()

    @pl.loop(1, rows)
    def _(k):
        along_in(k).wait_recv()
        place = (mine + k) % rows
        across(place, lane).start()
        sideways(place, lane, 0).start()

    @pl.loop(0, rows)
    def _(k):
        place = (mine + k) % rows
        across(place, lane_across).wait_recv()
        sideways(place, lane_across, 1).start()

    @pl.loop(0, rows)
    def _(k):
        place = (mine + k) % rows
        sideways(place, lane_sibling, 0).wait_recv()
        sideways(place, lane_diagonal, 1).wait_recv()
        across(place, lane).wait_send()
        sideways(place, lane, 0).wait_send()
        sideways(place, lane_across, 1).wait_send()

    @pl.loop(1, rows)
    def _(k):
        along(k).wait_send()


def gather_sems(count):
    rows = count // 4
    return [pltpu.SemaphoreType.DMA((rows,))] * 4 + [pltpu.SemaphoreType.DMA((2, rows))] * 2


def pair_copy(count, src, dst, send_sem, recv_sem, k):
    me = lax.axis_index("groups")
    chips = count // 2
    chip = (me // 2 + k) % chips
    other = sibling_of(me)
    return remote(
        src.at[chip * 2 + other % 2], dst.at[chip], send_sem.at[chip], recv_sem.at[chip],
        "groups", other,
    )


def chip_copy(count, src, dst, send_sem, recv_sem, k):
    me = lax.axis_index("groups")
    chips = count // 2
    chip = (me // 2 + k) % chips
    return remote(
        src.at[chip], dst.at[me // 2], send_sem.at[chip], recv_sem.at[me // 2],
        "groups", chip * 2 + me % 2,
    )


def chip_copy_in(count, src, dst, send_sem, recv_sem, k):
    me = lax.axis_index("groups")
    chips = count // 2
    chip = (me // 2 + k) % chips
    return remote(
        src.at[chip], dst.at[chip], send_sem.at[chip], recv_sem.at[chip],
        "groups", chip * 2 + me % 2,
    )


def reduce_chunks(count, part, pair, out, into, total, sems):
    pair_send, pair_recv, chip_send, chip_recv = sems
    me = lax.axis_index("groups")
    chips = count // 2
    mine = me // 2

    @pl.loop(1, chips + 1)
    def _(k):
        pair_copy(count, part, pair, pair_send, pair_recv, k).start()

    @pl.loop(1, chips)
    def _(k):
        chip = (mine + k) % chips
        pair_copy(count, part, pair, pair_send, pair_recv, k).wait_recv()
        out[chip] = (part[chip * 2 + me % 2] + pair[chip]).astype(jnp.bfloat16)
        chip_copy(count, out, into, chip_send, chip_recv, k).start()

    pair_copy(count, part, pair, pair_send, pair_recv, chips).wait_recv()
    total[...] = part[me] + pair[mine]

    @pl.loop(1, chips)
    def _(k):
        chip = (mine + k) % chips
        chip_copy_in(count, out, into, chip_send, chip_recv, k).wait_recv()
        total[...] += into[chip].astype(jnp.float32)

    @pl.loop(1, chips + 1)
    def _(k):
        pair_copy(count, part, pair, pair_send, pair_recv, k).wait_send()

    @pl.loop(1, chips)
    def _(k):
        chip_copy(count, out, into, chip_send, chip_recv, k).wait_send()


def reduce_scratch(count, rows, columns):
    chips = count // 2
    return [
        pltpu.VMEM((count, rows, columns), jnp.float32),
        pltpu.VMEM((chips, rows, columns), jnp.float32),
        pltpu.VMEM((chips, rows, columns), jnp.bfloat16),
        pltpu.VMEM((chips, rows, columns), jnp.bfloat16),
        pltpu.VMEM((rows, columns), jnp.float32),
    ] + [pltpu.SemaphoreType.DMA((chips,))] * 4


def project_kernel(
    count, hidden, weight, cosine, sine, queries, news,
    part, pair, out, into, total, ps, pr, cs, cr, *gather,
):
    me = lax.axis_index("groups")
    rows, wide = part.shape[1:]
    heads = weight.shape[1] // wide
    tile = 2 * HD
    per = wide // tile

    @pl.loop(0, heads * per)
    def _(t):
        head = t // per
        here = pl.ds(pl.multiple_of(t * tile, tile), tile)
        there = pl.ds(pl.multiple_of((t % per) * tile, tile), tile)
        piece = jnp.dot(hidden[...], weight[:, here], preferred_element_type=jnp.float32)
        for block in range(count // heads):
            part[block * heads + head, :, there] = piece[block * rows : (block + 1) * rows]

    greet_pairs(count)
    reduce_chunks(count, part, pair, out, into, total, (ps, pr, cs, cr))
    for index in range(GQ + 1):
        vector = total[:, index * HD : (index + 1) * HD]
        turned = vector * cosine[...] + pltpu.roll(vector, HD // 2, 1) * sine[...]
        if index < GQ:
            queries[me, :, index * HD : (index + 1) * HD] = turned.astype(jnp.bfloat16)
        else:
            news[:, :HD] = turned.astype(jnp.bfloat16)
    news[:, HD:] = total[:, (GQ + 1) * HD :].astype(jnp.bfloat16)
    gather_chunks(count, queries, gather)


def attend_kernel(
    queries, cache_keys, cache_values, cosine, sine, news, key_pos, listed, numer, stats,
    keys, values, mask,
):
    capacity = cache_keys.shape[0]
    fresh = news.shape[0]
    blocks, rows = queries.shape[0], queries.shape[2]
    span = keys.shape[0]
    for block in range(capacity // BLK):
        here = slice(block * BLK, (block + 1) * BLK)
        vector = cache_keys[here, :].astype(jnp.float32)
        turned = (
            vector * cosine[block : block + 1, :]
            + pltpu.roll(vector, HD // 2, 1) * sine[block : block + 1, :]
        )
        keys[here, :] = turned.astype(jnp.bfloat16)
    values[:, HD:] = jnp.ones((span, HD), jnp.bfloat16)
    values[:capacity, :HD] = cache_values[...]
    keys[capacity : capacity + fresh, :] = news[:, :HD]
    values[capacity : capacity + fresh, :HD] = news[:, HD:]
    if span > capacity + fresh:
        rest = span - capacity - fresh
        keys[capacity + fresh :, :] = jnp.zeros((rest, HD), jnp.bfloat16)
        values[capacity + fresh :, :HD] = jnp.zeros((rest, HD), jnp.bfloat16)
    mask[...] = jnp.where(key_pos[0] <= listed[...], 0.0, masked_score)
    scale = HD ** (-0.5)
    lanes = lax.broadcasted_iota(jnp.int32, (blocks * rows, HD), 1)
    summary = jnp.zeros((blocks * rows, HD), jnp.float32)
    for index in range(GQ):
        here = slice(index * HD, (index + 1) * HD)
        query = queries[:, 0, :, here].reshape(blocks * rows, HD)
        scores = lax.dot_general(
            query, keys[...], (((1,), (1,)), ((), ())), preferred_element_type=jnp.float32
        )
        scores = scores + mask[...]
        peak = jnp.max(scores, axis=1, keepdims=True)
        weights = jnp.exp((scores - jnp.maximum(peak, -1e25)) * scale).astype(jnp.bfloat16)
        both = jnp.dot(weights, values[...], preferred_element_type=jnp.float32)
        totals = both[:, HD:]
        some = totals > 0.0
        safe = jnp.where(some, totals, 1.0)
        numer[:, 0, :, here] = (both[:, :HD] / safe).reshape(blocks, rows, HD)
        level = jnp.where(some, peak * scale + jnp.log(safe), masked_score)
        summary = jnp.where(lanes == index, level, summary)
    stats[:, 0] = summary.reshape(blocks, rows, HD)


def combine_kernel(
    count, numer, stats, heads_out,
    pair, pair_level, out, out_level, into, into_level, total, total_level,
    ps, pr, pls, plr, cs, cr, cls, clr, *gather,
):
    me = lax.axis_index("groups")
    chips = count // 2
    mine = me // 2
    greet_pairs(count)

    @pl.loop(1, chips + 1)
    def _(k):
        pair_copy(count, stats, pair_level, pls, plr, k).start()
        pair_copy(count, numer, pair, ps, pr, k).start()

    def merged(k, chip):
        slot = chip * 2 + me % 2
        pair_copy(count, stats, pair_level, pls, plr, k).wait_recv()
        pair_copy(count, numer, pair, ps, pr, k).wait_recv()
        one, two = stats[slot], pair_level[chip]
        top = jnp.maximum(one, two)
        one, two = jnp.exp(one - top), jnp.exp(two - top)
        both = one + two
        one, two = one / both, two / both
        parts = []
        for index in range(GQ):
            here = slice(index * HD, (index + 1) * HD)
            parts.append(
                numer[slot, :, here] * one[:, index : index + 1]
                + pair[chip, :, here] * two[:, index : index + 1]
            )
        return parts, top + jnp.log(both)

    @pl.loop(1, chips)
    def _(k):
        chip = (mine + k) % chips
        parts, level = merged(k, chip)
        out_level[chip] = level
        chip_copy(count, out_level, into_level, cls, clr, k).start()
        for index in range(GQ):
            out[chip, :, index * HD : (index + 1) * HD] = parts[index].astype(jnp.bfloat16)
        chip_copy(count, out, into, cs, cr, k).start()

    parts, level = merged(chips, mine)
    for index in range(GQ):
        total[:, index * HD : (index + 1) * HD] = parts[index]
    total_level[...] = level

    @pl.loop(1, chips)
    def _(k):
        chip = (mine + k) % chips
        chip_copy_in(count, out_level, into_level, cls, clr, k).wait_recv()
        chip_copy_in(count, out, into, cs, cr, k).wait_recv()
        one, two = total_level[...], into_level[chip]
        top = jnp.maximum(one, two)
        one, two = jnp.exp(one - top), jnp.exp(two - top)
        both = one + two
        total_level[...] = top + jnp.log(both)
        one, two = one / both, two / both
        for index in range(GQ):
            here = slice(index * HD, (index + 1) * HD)
            total[:, here] = (
                total[:, here] * one[:, index : index + 1]
                + into[chip, :, here].astype(jnp.float32) * two[:, index : index + 1]
            )

    heads_out[me] = total[...].astype(jnp.bfloat16)
    gather_chunks(count, heads_out, gather)

    @pl.loop(1, chips + 1)
    def _(k):
        pair_copy(count, stats, pair_level, pls, plr, k).wait_send()
        pair_copy(count, numer, pair, ps, pr, k).wait_send()

    @pl.loop(1, chips)
    def _(k):
        chip_copy(count, out_level, into_level, cls, clr, k).wait_send()
        chip_copy(count, out, into, cs, cr, k).wait_send()


def output_kernel(
    count, splits, wanted, heads_out, hidden, gain, out_weight, next_weight, hidden_out, next_out,
    out_held, next_held, load_sem, terms, term_send, term_recv, square, square_send, square_recv,
    scaled, left, part, pair, out, into, total, ps, pr, cs, cr,
):
    me = lax.axis_index("groups")
    my_split = lax.axis_index("heads")
    chunk = heads_out.shape[1]
    height = hidden.shape[0]
    kv_local = out_held.shape[0] // heads_out.shape[2]
    depth = heads_out.shape[2]
    loads = [
        pltpu.make_async_copy(out_weight, out_held, load_sem.at[0]),
        pltpu.make_async_copy(next_weight, next_held, load_sem.at[1]),
    ]
    for load in loads:
        load.start()

    barrier = pltpu.get_barrier_semaphore()

    @pl.loop(1, count)
    def _(k):
        pl.semaphore_signal(
            barrier, inc=1, device_id={"groups": (me + k) % count}, device_id_type=MESH
        )

    @pl.loop(1, splits)
    def _(k):
        pl.semaphore_signal(
            barrier, inc=1, device_id={"heads": (my_split + k) % splits}, device_id_type=MESH
        )

    loads[0].wait()
    term = jnp.zeros((height, hidden.shape[1]), jnp.float32)
    for head in range(kv_local):
        block = heads_out[...].reshape(count // kv_local, kv_local, chunk, depth)[:, head]
        term += jnp.dot(
            block.reshape(height, depth),
            out_held[head * depth : (head + 1) * depth, :],
            preferred_element_type=jnp.float32,
        )
    terms[my_split] = term.astype(jnp.bfloat16)
    pl.semaphore_wait(barrier, count - 1 + splits - 1)

    def share(k):
        return remote(
            terms.at[my_split], terms.at[my_split], term_send.at[k], term_recv.at[my_split],
            "heads", (my_split + k) % splits,
        )

    def share_in(k):
        other = (my_split + k) % splits
        return remote(
            terms.at[other], terms.at[other], term_send.at[k], term_recv.at[other], "heads", other
        )

    @pl.loop(1, splits)
    def _(k):
        share(k).start()

    @pl.loop(1, splits)
    def _(k):
        share_in(k).wait_recv()

    attended = terms[0].astype(jnp.float32)
    for index in range(1, splits):
        attended += terms[index].astype(jnp.float32)
    resid = hidden[...].astype(jnp.float32) + attended
    hidden_out[...] = resid.astype(jnp.bfloat16)
    column = jnp.sum(resid * resid, axis=1, keepdims=True)
    diagonal = lax.broadcasted_iota(jnp.int32, (height, height), 0) == lax.broadcasted_iota(
        jnp.int32, (height, height), 1
    )
    line = jnp.sum(jnp.where(diagonal, column, 0.0), axis=0, keepdims=True)
    square[me] = jnp.broadcast_to(line, square.shape[1:])

    def spread(k):
        return remote(
            square.at[me], square.at[me], square_send.at[k], square_recv.at[me],
            "groups", (me + k) % count,
        )

    def spread_in(k):
        other = (me + k) % count
        return remote(
            square.at[other], square.at[other], square_send.at[k], square_recv.at[other],
            "groups", other,
        )

    @pl.loop(1, count)
    def _(k):
        spread(k).start()

    scaled[...] = resid * gain[...]

    @pl.loop(1, count)
    def _(k):
        spread_in(k).wait_recv()

    line = jnp.sum(square[...], axis=0)[0:1, :]
    squares = jnp.sum(jnp.where(diagonal, line, 0.0), axis=1, keepdims=True)
    width = hidden.shape[1] * count
    scaled[...] = scaled[...] * lax.rsqrt(squares / width + epsilon)

    held_rows = left.shape[1]
    own_rows = wanted
    left[...] = jnp.zeros_like(left)
    for index in range(count):
        first = (index // kv_local) * chunk + (index % kv_local) * own_rows
        left[index, :own_rows, :] = scaled[first : first + own_rows, :]
    lhs = left[...].reshape(count * held_rows, hidden.shape[1]).astype(jnp.bfloat16)
    loads[1].wait()
    tile = 2 * HD

    @pl.loop(0, next_held.shape[1] // tile)
    def _(t):
        here = pl.ds(pl.multiple_of(t * tile, tile), tile)
        piece = jnp.dot(lhs, next_held[:, here], preferred_element_type=jnp.float32)
        part[:, :, here] = piece.reshape(count, held_rows, tile)

    reduce_chunks(count, part, pair, out, into, total, (ps, pr, cs, cr))
    next_out[...] = total[...].astype(jnp.bfloat16)

    @pl.loop(1, splits)
    def _(k):
        share(k).wait_send()

    @pl.loop(1, count)
    def _(k):
        spread(k).wait_send()


def layout(
    owner_index, group_lengths, group_owner, group_start, listed_rows, cap_blocks, block_rows
):
    block_len = group_lengths // block_rows
    holder = (group_owner == owner_index).astype(jnp.int32)
    held_blocks = holder * block_len
    offset = jnp.cumsum(held_blocks) - held_blocks
    block_ids = jnp.arange(cap_blocks)[:, None]
    member = (
        (holder[None, :] == 1)
        & (block_ids >= offset[None, :])
        & (block_ids < offset[None, :] + block_len[None, :])
    ).astype(jnp.int32)
    shift_blk = jnp.sum(member * group_start[None, :], axis=1)
    begin_blk = jnp.sum(
        member * (group_start[None, :] + (block_ids - offset[None, :]) * block_rows), axis=1
    )
    live_blk = jnp.sum(member, axis=1) > 0
    inside = jnp.arange(block_rows)[None, :]
    key_pos = (begin_blk[:, None] + inside).reshape(-1)
    listed_hit = jnp.any(key_pos[:, None] == listed_rows[None, :], axis=1)
    key_live = jnp.repeat(live_blk, block_rows) & jnp.logical_not(listed_hit)
    return (jnp.where(key_live, key_pos, NEVER), shift_blk)


VMEM = pl.BlockSpec(memory_space=pltpu.VMEM)
ANY = pl.BlockSpec(memory_space=pl.ANY)


def on_device(
    count,
    splits,
    hidden_rows,
    qkv_weight,
    out_weight,
    norm_gain,
    next_weight,
    cache_keys,
    cache_values,
    group_lengths,
    group_owner,
    group_start,
    listed_rows,
):
    me = lax.axis_index("groups")
    row_count, model_part = hidden_rows.shape
    depth = GQ * HD
    kv_local = out_weight.shape[0] // depth
    wide = (GQ + 2) * HD
    blocks = count // kv_local
    own = row_count // blocks
    chunk = round_up(own, 16)
    height = blocks * chunk
    capacity = cache_keys.shape[0]

    def padded(array):
        if chunk == own:
            return array
        array = array.reshape((blocks, own) + array.shape[1:])
        fill = [(0, 0), (0, chunk - own)] + [(0, 0)] * (array.ndim - 2)
        return jnp.pad(array, fill).reshape((height,) + array.shape[2:])

    hidden = padded(hidden_rows)
    listed = padded(listed_rows)
    own_pos = lax.dynamic_slice_in_dim(listed, (me // kv_local) * chunk, chunk)
    own_cos, own_sin = full_angles(own_pos)
    queries, news = pl.pallas_call(
        functools.partial(project_kernel, count),
        out_shape=(
            jax.ShapeDtypeStruct((count, chunk, depth), jnp.bfloat16),
            jax.ShapeDtypeStruct((chunk, 2 * HD), jnp.bfloat16),
        ),
        in_specs=[VMEM] * 4,
        out_specs=(VMEM, VMEM),
        scratch_shapes=reduce_scratch(count, chunk, wide) + gather_sems(count),
        compiler_params=pltpu.CompilerParams(
            collective_id=0, has_side_effects=True, vmem_limit_bytes=LIMIT
        ),
        name="project",
    )(hidden, qkv_weight, own_cos, own_sin)

    key_pos, key_shift = layout(
        me, group_lengths, group_owner, group_start, listed_rows, capacity // BLK, BLK
    )
    store_cos, store_sin = full_angles(key_shift)
    span = round_up(capacity + chunk, BLK)
    fresh_pos = jnp.where(jnp.arange(chunk) < own, own_pos, NEVER)
    fresh_pos = jnp.where(
        jnp.arange(kv_local)[:, None] == me % kv_local, fresh_pos[None, :], NEVER
    )
    all_pos = jnp.concatenate(
        [
            jnp.broadcast_to(key_pos[None, :], (kv_local, capacity)),
            fresh_pos,
            jnp.full((kv_local, span - capacity - chunk), NEVER, jnp.int32),
        ],
        axis=1,
    )[:, None, :]
    steady = lambda shape: pl.BlockSpec(shape, lambda h: (0,) * len(shape))
    numer, stats = pl.pallas_call(
        attend_kernel,
        grid=(kv_local,),
        out_shape=(
            jax.ShapeDtypeStruct((blocks, kv_local, chunk, depth), jnp.float32),
            jax.ShapeDtypeStruct((blocks, kv_local, chunk, HD), jnp.float32),
        ),
        in_specs=[
            pl.BlockSpec((blocks, 1, chunk, depth), lambda h: (0, h, 0, 0)),
            pl.BlockSpec((capacity, HD), lambda h: (0, h)),
            pl.BlockSpec((capacity, HD), lambda h: (0, h)),
            steady(store_cos.shape),
            steady(store_sin.shape),
            steady((chunk, 2 * HD)),
            pl.BlockSpec((1, 1, span), lambda h: (h, 0, 0)),
            steady((height, 1)),
        ],
        out_specs=(
            pl.BlockSpec((blocks, 1, chunk, depth), lambda h: (0, h, 0, 0)),
            pl.BlockSpec((blocks, 1, chunk, HD), lambda h: (0, h, 0, 0)),
        ),
        scratch_shapes=[
            pltpu.VMEM((span, HD), jnp.bfloat16),
            pltpu.VMEM((span, 2 * HD), jnp.bfloat16),
            pltpu.VMEM((height, span), jnp.float32),
        ],
        compiler_params=pltpu.CompilerParams(vmem_limit_bytes=LIMIT),
        name="attend",
    )(
        queries.reshape(blocks, kv_local, chunk, depth),
        cache_keys,
        cache_values,
        store_cos,
        store_sin,
        news,
        all_pos,
        listed[:, None],
    )

    chips = count // 2
    heads_out = pl.pallas_call(
        functools.partial(combine_kernel, count),
        out_shape=jax.ShapeDtypeStruct((count, chunk, depth), jnp.bfloat16),
        in_specs=[VMEM] * 2,
        out_specs=VMEM,
        scratch_shapes=[
            pltpu.VMEM((chips, chunk, depth), jnp.float32),
            pltpu.VMEM((chips, chunk, HD), jnp.float32),
            pltpu.VMEM((chips, chunk, depth), jnp.bfloat16),
            pltpu.VMEM((chips, chunk, HD), jnp.float32),
            pltpu.VMEM((chips, chunk, depth), jnp.bfloat16),
            pltpu.VMEM((chips, chunk, HD), jnp.float32),
            pltpu.VMEM((chunk, depth), jnp.float32),
            pltpu.VMEM((chunk, HD), jnp.float32),
        ]
        + [pltpu.SemaphoreType.DMA((chips,))] * 8
        + gather_sems(count),
        compiler_params=pltpu.CompilerParams(
            collective_id=1, has_side_effects=True, vmem_limit_bytes=LIMIT
        ),
        name="combine",
    )(numer.reshape(count, chunk, depth), stats.reshape(count, chunk, HD))

    held = round_up(row_count // count, 16)
    next_wide = next_weight.shape[1]
    hidden_out, next_out = pl.pallas_call(
        functools.partial(output_kernel, count, splits, row_count // count),
        out_shape=(
            jax.ShapeDtypeStruct((height, model_part), jnp.bfloat16),
            jax.ShapeDtypeStruct((held, next_wide), jnp.bfloat16),
        ),
        in_specs=[VMEM, VMEM, VMEM, ANY, ANY],
        out_specs=(VMEM, VMEM),
        scratch_shapes=[
            pltpu.VMEM(out_weight.shape, jnp.bfloat16),
            pltpu.VMEM(next_weight.shape, jnp.bfloat16),
            pltpu.SemaphoreType.DMA((2,)),
            pltpu.VMEM((splits, height, model_part), jnp.bfloat16),
            pltpu.SemaphoreType.DMA((splits,)),
            pltpu.SemaphoreType.DMA((splits,)),
            pltpu.VMEM((count, 8, height), jnp.float32),
            pltpu.SemaphoreType.DMA((count,)),
            pltpu.SemaphoreType.DMA((count,)),
            pltpu.VMEM((height, model_part), jnp.float32),
            pltpu.VMEM((count, held, model_part), jnp.float32),
        ]
        + reduce_scratch(count, held, next_wide),
        compiler_params=pltpu.CompilerParams(
            collective_id=2, has_side_effects=True, vmem_limit_bytes=LIMIT
        ),
        name="output",
    )(heads_out, hidden, norm_gain[None, :], out_weight, next_weight)
    if chunk != own:
        hidden_out = hidden_out.reshape(blocks, chunk, model_part)[:, :own]
        hidden_out = hidden_out.reshape(row_count, model_part)
    return (hidden_out, next_out[: row_count // count])


def solution(mesh):
    in_specs = (
        P(None, "groups"),
        P("groups", "heads"),
        P("heads", "groups"),
        P("groups"),
        P("groups", "heads"),
        P("groups", "heads"),
        P("groups", "heads"),
        P(),
        P(),
        P(),
        P(),
    )
    out_specs = (P(None, "groups"), P("groups", "heads"))
    return jax.shard_map(
        functools.partial(on_device, mesh.shape["groups"], mesh.shape["heads"]),
        mesh=mesh,
        in_specs=in_specs,
        out_specs=out_specs,
        check_vma=False,
    )
```

time: 529 us -> 193 us (0.36)
  blocking collectives: 251 us -> 0 us
  Pallas kernels: 0 us -> 180 us
  waiting for transfers between devices: 121 us -> 0 us
  matrix products: 51.8 us -> 0 us
  local copies, waits for them, and re-layouts: 40.3 us -> 5.43 us
  starting transfers between devices: 28.5 us -> 0 us
  between operations: 15.4 us -> 0.73 us
  other arithmetic: 19.1 us -> 6.46 us
    pallas_call x0 -> x4, Pallas kernels: none -> 180 us  [the longest x1 59.6 us: on_device(): pl.pallas_call(functools.partial(output_kernel, count, splits, row_count...]
    unnamed x2 -> x0, blocking collectives: 122 us -> none
    psum x2 -> x0, blocking collectives: 79.9 us -> none  [the longest x1 59.5 us: on_device(): lax.psum((numerator * factor[..., None], totals * factor), 'groups')]
    psum x2 -> x0, waiting for transfers between devices: 76.1 us -> none  [the longest x1 53.6 us: on_device(): lax.psum((numerator * factor[..., None], totals * factor), 'groups')]
    dot_general x35 -> x0, matrix products: 51.8 us -> none  [the longest x16 24.6 us: on_device(): jnp.einsum('rgd,kd->rgk', query_block, key_block, preferred_element_type=...]
    pmax x1 -> x0, blocking collectives: 49.1 us -> none  [on_device(): highest = lax.pmax(peaks, 'groups')]
    unnamed x151 -> x2, local copies, waits for them, and re-layouts: 32.4 us -> 3.21 us
    unnamed x8 -> x0, starting transfers between devices: 28.2 us -> none
  transfers between devices with their start and end apart: 11 -> 0, of which waited for: 5 -> 0; matrix products, arithmetic and copies ran while one was open for 4% -> 0% of each run, Pallas kernels for 0% -> 0%
where the time goes in v1:
time: 193 us
  Pallas kernels  180 us (93%)
  other arithmetic  6.46 us (3%)
  local copies, waits for them, and re-layouts  5.43 us (3%)
    pallas_call x1, Pallas kernels, on_device(): pl.pallas_call(functools.partial(output_kernel, count, splits, row_count...  59.6 us
    pallas_call x1, Pallas kernels, on_device(): pl.pallas_call(functools.partial(project_kernel, count), out_shape=(jax.S...  54.1 us
    pallas_call x1, Pallas kernels, on_device(): pl.pallas_call(functools.partial(combine_kernel, count), out_shape=jax.Sh...  51.9 us
    pallas_call x1, Pallas kernels, on_device(): pl.pallas_call(attend_kernel, grid=(kv_local,), out_shape=(jax.ShapeDtype...  14.7 us

profile of v1, /device:TPU:10, one launch (start us, length us, event | category | flops | bytes accessed | tf_op | source)
XLA Modules:
  0.0 192.9 jit_solution(6199350739868947357)
XLA Ops:
  0.7 0.7 fusion.5
  1.3 0.8 compare_select_fusion
  2.1 0.1 broadcast_select_fusion
  2.2 0.7 fusion.7
  2.9 0.1 pad.2.clone
  2.9 0.1 copy.16
  3.1 0.1 reduce
  3.2 0.7 fusion.8
  3.9 0.8 select_reduce_fusion
  4.7 0.1 add_bitcast_fusion
  4.8 0.8 compare_reduce_fusion
  5.6 0.1 fusion.3
  5.7 0.6 broadcast_in_dim.74.key_pos
  6.3 0.1 fusion.4
  6.4 0.7 pad_maximum_fusion.2
  7.1 0.2 fusion
  7.3 0.7 pad_maximum_fusion
  7.9 1.4 copy.17.listed
  9.4 54.1 %project.1 = (bf16[16,48,1024]{2,1,0:T(8,128)(2,1)}, bf16[48,256]{1,0:T(8,128)(2,1)}) custom-call(bf16[192,512]{1,0:T(8,128)(2,1)} %hidden.3, bf16[512,5120]{1,0:T(8,128)(2,1)} %weight.1, f32[48,128]{1,0:T(8,128)} %get-tuple-element.29.cosine, f32[48,128]{1,0:T(8,128)} %get-tuple-element.30.sine), custom_call_target="tpu_custom_call" | custom-call | tf_op jit(solution)/shard_map/project/pallas_call | solution.py:590
  63.5 14.7 %attend.1 = (f32[4,4,48,1024]{3,2,1,0:T(8,128)}, f32[4,4,48,128]{3,2,1,0:T(8,128)}) custom-call(bf16[4,4,48,1024]{3,2,1,0:T(8,128)(2,1)} %bitcast.17, bf16[768,512]{1,0:T(8,128)(2,1)} %cache_keys.1, bf16[768,512]{1,0:T(8,128)(2,1)} %cache_values.1, f32[6,128]{1,0:T(8,128)} %get-tuple-element.31.cosine, f32[6,128]{1,0:T(8,128)} %get-tuple-element.32.sine, ...), custom_call_target="tpu_custom_call" | custom-call | tf_op jit(solution)/shard_map/attend/pallas_call | solution.py:623
  78.1 51.9 %combine.1.heads_out = bf16[16,48,1024]{2,1,0:T(8,128)(2,1)} custom-call(f32[16,48,1024]{2,1,0:T(8,128)} %bitcast.16, f32[16,48,128]{2,1,0:T(8,128)} %bitcast.18), custom_call_target="tpu_custom_call" | custom-call | tf_op jit(solution)/shard_map/combine/pallas_call | solution.py:663
  130.1 59.6 %output.1 = (bf16[192,512]{1,0:T(8,128)(2,1)}, bf16[16,5120]{1,0:T(8,128)(2,1)}) custom-call(bf16[16,48,1024]{2,1,0:T(8,128)(2,1)} %combine.1.heads_out, bf16[192,512]{1,0:T(8,128)(2,1)} %hidden.3, f32[1,512]{1,0:T(1,128)} %bitcast.21, bf16[4096,512]{1,0:T(8,128)(2,1)} %out_weight.1, bf16[512,5120]{1,0:T(8,128)(2,1)} %next_weight.1), custom_call_target="tpu_custom_call" | custom-call | tf_op jit(solution)/shard_map/output/pallas_call | solution.py:688
  189.7 1.6 copy.20
  191.3 1.6 copy.21
  (8 shorter events, 0.1 us)

commit v2 on v1

--- a/solution.py
+++ b/solution.py
@@ -55,20 +55,19 @@
     return me + 2 - 4 * ((me // 2) % 2)
 
 
-def greet_pairs(count):
+def greet(count):
     me = lax.axis_index("groups")
-    chips = count // 2
+    rows = count // 4
     barrier = pltpu.get_barrier_semaphore()
-    pl.semaphore_signal(
-        barrier, inc=1, device_id={"groups": sibling_of(me)}, device_id_type=MESH
-    )
-
-    @pl.loop(1, chips)
-    def _(k):
-        other = ((me // 2 + k) % chips) * 2 + me % 2
+    for other in (sibling_of(me), across_of(me)):
         pl.semaphore_signal(barrier, inc=1, device_id={"groups": other}, device_id_type=MESH)
 
-    pl.semaphore_wait(barrier, chips)
+    @pl.loop(1, rows)
+    def _(k):
+        other = ((me // 4 + k) % rows) * 4 + me % 4
+        pl.semaphore_signal(barrier, inc=1, device_id={"groups": other}, device_id_type=MESH)
+
+    pl.semaphore_wait(barrier, rows + 1)
 
 
 def gather_chunks(count, out, sems):
@@ -153,86 +152,138 @@
     return [pltpu.SemaphoreType.DMA((rows,))] * 4 + [pltpu.SemaphoreType.DMA((2, rows))] * 2
 
 
-def pair_copy(count, src, dst, send_sem, recv_sem, k):
+def whole_chunk(part, chip, core):
+    return part.at[chip * 2 + core]
+
+
+def half_chunk(part, chip, core):
+    half = part.shape[2] // 2
+    return part.at[chip, :, pl.ds(pl.multiple_of(core * half, HD), half)]
+
+
+def reduce_chunks(count, fields, merge, view):
     me = lax.axis_index("groups")
-    chips = count // 2
-    chip = (me // 2 + k) % chips
-    other = sibling_of(me)
-    return remote(
-        src.at[chip * 2 + other % 2], dst.at[chip], send_sem.at[chip], recv_sem.at[chip],
-        "groups", other,
-    )
-
-
-def chip_copy(count, src, dst, send_sem, recv_sem, k):
-    me = lax.axis_index("groups")
-    chips = count // 2
-    chip = (me // 2 + k) % chips
-    return remote(
-        src.at[chip], dst.at[me // 2], send_sem.at[chip], recv_sem.at[me // 2],
-        "groups", chip * 2 + me % 2,
-    )
-
-
-def chip_copy_in(count, src, dst, send_sem, recv_sem, k):
-    me = lax.axis_index("groups")
-    chips = count // 2
-    chip = (me // 2 + k) % chips
-    return remote(
-        src.at[chip], dst.at[chip], send_sem.at[chip], recv_sem.at[chip],
-        "groups", chip * 2 + me % 2,
-    )
-
-
-def reduce_chunks(count, part, pair, out, into, total, sems):
-    pair_send, pair_recv, chip_send, chip_recv = sems
-    me = lax.axis_index("groups")
-    chips = count // 2
-    mine = me // 2
-
-    @pl.loop(1, chips + 1)
-    def _(k):
-        pair_copy(count, part, pair, pair_send, pair_recv, k).start()
-
-    @pl.loop(1, chips)
-    def _(k):
-        chip = (mine + k) % chips
-        pair_copy(count, part, pair, pair_send, pair_recv, k).wait_recv()
-        out[chip] = (part[chip * 2 + me % 2] + pair[chip]).astype(jnp.bfloat16)
-        chip_copy(count, out, into, chip_send, chip_recv, k).start()
-
-    pair_copy(count, part, pair, pair_send, pair_recv, chips).wait_recv()
-    total[...] = part[me] + pair[mine]
-
-    @pl.loop(1, chips)
-    def _(k):
-        chip = (mine + k) % chips
-        chip_copy_in(count, out, into, chip_send, chip_recv, k).wait_recv()
-        total[...] += into[chip].astype(jnp.float32)
-
-    @pl.loop(1, chips + 1)
-    def _(k):
-        pair_copy(count, part, pair, pair_send, pair_recv, k).wait_send()
-
-    @pl.loop(1, chips)
-    def _(k):
-        chip_copy(count, out, into, chip_send, chip_recv, k).wait_send()
-
-
-def reduce_scratch(count, rows, columns):
-    chips = count // 2
-    return [
-        pltpu.VMEM((count, rows, columns), jnp.float32),
-        pltpu.VMEM((chips, rows, columns), jnp.float32),
-        pltpu.VMEM((chips, rows, columns), jnp.bfloat16),
-        pltpu.VMEM((chips, rows, columns), jnp.bfloat16),
-        pltpu.VMEM((rows, columns), jnp.float32),
-    ] + [pltpu.SemaphoreType.DMA((chips,))] * 4
+    rows = count // 4
+    core, side, mine = me % 2, (me // 2) % 2, me // 4
+    sibling, opposite = sibling_of(me), across_of(me)
+
+    def pair_copy(field, chip):
+        part, pair, sems = field[0], field[1], field[6]
+        return remote(
+            view(part, chip, sibling % 2), pair.at[chip], sems[0].at[chip], sems[1].at[chip],
+            "groups", sibling,
+        )
+
+    def across(field, place):
+        sems = field[6]
+        return remote(
+            field[2].at[place], field[3].at[place], sems[2].at[place], sems[3].at[place],
+            "groups", opposite,
+        )
+
+    def along(field, place, slot):
+        sems = field[6]
+        return remote(
+            field[4].at[place], field[5].at[slot], sems[4].at[place], sems[5].at[slot],
+            "groups", place * 4 + me % 4,
+        )
+
+    def on_chip(chip):
+        for field in fields:
+            pair_copy(field, chip).wait_recv()
+        return merge(
+            [view(field[0], chip, core)[...] for field in fields],
+            [field[1][chip] for field in fields],
+        )
+
+    for wanted in (1 - side, side):
+
+        @pl.loop(1, rows + 1)
+        def _(k):
+            for field in fields:
+                pair_copy(field, ((mine + k) % rows) * 2 + wanted).start()
+
+    @pl.loop(1, rows + 1)
+    def _(k):
+        place = (mine + k) % rows
+        for field, value in zip(fields, on_chip(place * 2 + 1 - side)):
+            field[2][place] = value.astype(field[2].dtype)
+            across(field, place).start()
+
+    def on_row(place):
+        value = on_chip(place * 2 + side)
+        for field in fields:
+            across(field, place).wait_recv()
+        return merge(value, [field[3][place].astype(jnp.float32) for field in fields])
+
+    @pl.loop(1, rows)
+    def _(k):
+        place = (mine + k) % rows
+        for field, value in zip(fields, on_row(place)):
+            field[4][place] = value.astype(field[4].dtype)
+            along(field, place, mine).start()
+
+    value = on_row(mine)
+    for k in range(1, rows):
+        place = (mine + k) % rows
+        for field in fields:
+            along(field, place, place).wait_recv()
+        value = merge(value, [field[5][place].astype(jnp.float32) for field in fields])
+
+    @pl.loop(0, count // 2)
+    def _(chip):
+        for field in fields:
+            pair_copy(field, chip).wait_send()
+
+    @pl.loop(0, rows)
+    def _(place):
+        for field in fields:
+            across(field, place).wait_send()
+
+    @pl.loop(1, rows)
+    def _(k):
+        for field in fields:
+            along(field, (mine + k) % rows, mine).wait_send()
+
+    return value
+
+
+def added(one, two):
+    return [one[0] + two[0]]
+
+
+def merged(one, two):
+    top = jnp.maximum(one[1], two[1])
+    first, second = jnp.exp(one[1] - top), jnp.exp(two[1] - top)
+    both = first + second
+    first, second = first / both, second / both
+    parts = []
+    for index in range(GQ):
+        here = slice(index * HD, (index + 1) * HD)
+        parts.append(
+            one[0][:, here] * first[:, index : index + 1]
+            + two[0][:, here] * second[:, index : index + 1]
+        )
+    return [jnp.concatenate(parts, axis=1), top + jnp.log(both)]
+
+
+def reduce_scratch(count, rows, columns, dtype):
+    place = pltpu.VMEM((count // 4, rows, columns), dtype)
+    return [pltpu.VMEM((count // 2, rows, columns), jnp.float32), place, place, place, place] + [
+        pltpu.SemaphoreType.DMA((count // 2,))
+    ] * 2 + [pltpu.SemaphoreType.DMA((count // 4,))] * 4
+
+
+FIELD = 11
+
+
+def field_of(part, scratch):
+    return (part, *scratch[:5], scratch[5:FIELD])
 
 
 def project_kernel(
     count, hidden, weight, cosine, sine, queries, news,
-    part, pair, out, into, total, ps, pr, cs, cr, *gather,
+    part, *scratch,
 ):
     me = lax.axis_index("groups")
     rows, wide = part.shape[1:]
@@ -249,8 +300,8 @@
         for block in range(count // heads):
             part[block * heads + head, :, there] = piece[block * rows : (block + 1) * rows]
 
-    greet_pairs(count)
-    reduce_chunks(count, part, pair, out, into, total, (ps, pr, cs, cr))
+    greet(count)
+    (total,) = reduce_chunks(count, [field_of(part, scratch)], added, whole_chunk)
     for index in range(GQ + 1):
         vector = total[:, index * HD : (index + 1) * HD]
         turned = vector * cosine[...] + pltpu.roll(vector, HD // 2, 1) * sine[...]
@@ -259,7 +310,7 @@
         else:
             news[:, :HD] = turned.astype(jnp.bfloat16)
     news[:, HD:] = total[:, (GQ + 1) * HD :].astype(jnp.bfloat16)
-    gather_chunks(count, queries, gather)
+    gather_chunks(count, queries, scratch[FIELD:])
 
 
 def attend_kernel(
@@ -309,90 +360,19 @@
     stats[:, 0] = summary.reshape(blocks, rows, HD)
 
 
-def combine_kernel(
-    count, numer, stats, heads_out,
-    pair, pair_level, out, out_level, into, into_level, total, total_level,
-    ps, pr, pls, plr, cs, cr, cls, clr, *gather,
-):
+def combine_kernel(count, numer, stats, heads_out, *scratch):
     me = lax.axis_index("groups")
-    chips = count // 2
-    mine = me // 2
-    greet_pairs(count)
-
-    @pl.loop(1, chips + 1)
-    def _(k):
-        pair_copy(count, stats, pair_level, pls, plr, k).start()
-        pair_copy(count, numer, pair, ps, pr, k).start()
-
-    def merged(k, chip):
-        slot = chip * 2 + me % 2
-        pair_copy(count, stats, pair_level, pls, plr, k).wait_recv()
-        pair_copy(count, numer, pair, ps, pr, k).wait_recv()
-        one, two = stats[slot], pair_level[chip]
-        top = jnp.maximum(one, two)
-        one, two = jnp.exp(one - top), jnp.exp(two - top)
-        both = one + two
-        one, two = one / both, two / both
-        parts = []
-        for index in range(GQ):
-            here = slice(index * HD, (index + 1) * HD)
-            parts.append(
-                numer[slot, :, here] * one[:, index : index + 1]
-                + pair[chip, :, here] * two[:, index : index + 1]
-            )
-        return parts, top + jnp.log(both)
-
-    @pl.loop(1, chips)
-    def _(k):
-        chip = (mine + k) % chips
-        parts, level = merged(k, chip)
-        out_level[chip] = level
-        chip_copy(count, out_level, into_level, cls, clr, k).start()
-        for index in range(GQ):
-            out[chip, :, index * HD : (index + 1) * HD] = parts[index].astype(jnp.bfloat16)
-        chip_copy(count, out, into, cs, cr, k).start()
-
-    parts, level = merged(chips, mine)
-    for index in range(GQ):
-        total[:, index * HD : (index + 1) * HD] = parts[index]
-    total_level[...] = level
-
-    @pl.loop(1, chips)
-    def _(k):
-        chip = (mine + k) % chips
-        chip_copy_in(count, out_level, into_level, cls, clr, k).wait_recv()
-        chip_copy_in(count, out, into, cs, cr, k).wait_recv()
-        one, two = total_level[...], into_level[chip]
-        top = jnp.maximum(one, two)
-        one, two = jnp.exp(one - top), jnp.exp(two - top)
-        both = one + two
-        total_level[...] = top + jnp.log(both)
-        one, two = one / both, two / both
-        for index in range(GQ):
-            here = slice(index * HD, (index + 1) * HD)
-            total[:, here] = (
-                total[:, here] * one[:, index : index + 1]
-                + into[chip, :, here].astype(jnp.float32) * two[:, index : index + 1]
-            )
-
-    heads_out[me] = total[...].astype(jnp.bfloat16)
-    gather_chunks(count, heads_out, gather)
-
-    @pl.loop(1, chips + 1)
-    def _(k):
-        pair_copy(count, stats, pair_level, pls, plr, k).wait_send()
-        pair_copy(count, numer, pair, ps, pr, k).wait_send()
-
-    @pl.loop(1, chips)
-    def _(k):
-        chip_copy(count, out_level, into_level, cls, clr, k).wait_send()
-        chip_copy(count, out, into, cs, cr, k).wait_send()
+    greet(count)
+    fields = [field_of(numer, scratch), field_of(stats, scratch[FIELD:])]
+    total, _ = reduce_chunks(count, fields, merged, whole_chunk)
+    heads_out[me] = total.astype(jnp.bfloat16)
+    gather_chunks(count, heads_out, scratch[2 * FIELD :])
 
 
 def output_kernel(
     count, splits, wanted, heads_out, hidden, gain, out_weight, next_weight, hidden_out, next_out,
     out_held, next_held, load_sem, terms, term_send, term_recv, square, square_send, square_recv,
-    scaled, left, part, pair, out, into, total, ps, pr, cs, cr,
+    scaled, left, swap_out, swap_in, swap_sem, part, *scratch,
 ):
     me = lax.axis_index("groups")
     my_split = lax.axis_index("heads")
@@ -493,13 +473,16 @@
     width = hidden.shape[1] * count
     scaled[...] = scaled[...] * lax.rsqrt(squares / width + epsilon)
 
-    held_rows = left.shape[1]
-    own_rows = wanted
-    left[...] = jnp.zeros_like(left)
-    for index in range(count):
-        first = (index // kv_local) * chunk + (index % kv_local) * own_rows
-        left[index, :own_rows, :] = scaled[first : first + own_rows, :]
-    lhs = left[...].reshape(count * held_rows, hidden.shape[1]).astype(jnp.bfloat16)
+    held = left.shape[1]
+    if 2 * wanted == held and count * wanted == height:
+        lhs = scaled[...].astype(jnp.bfloat16)
+    else:
+        left[...] = jnp.zeros_like(left)
+        for index in range(count):
+            first = (index // kv_local) * chunk + (index % kv_local) * wanted
+            there = (index % 2) * wanted
+            left[index // 2, there : there + wanted, :] = scaled[first : first + wanted, :]
+        lhs = left[...].reshape(count // 2 * held, hidden.shape[1]).astype(jnp.bfloat16)
     loads[1].wait()
     tile = 2 * HD
 
@@ -507,10 +490,24 @@
     def _(t):
         here = pl.ds(pl.multiple_of(t * tile, tile), tile)
         piece = jnp.dot(lhs, next_held[:, here], preferred_element_type=jnp.float32)
-        part[:, :, here] = piece.reshape(count, held_rows, tile)
-
-    reduce_chunks(count, part, pair, out, into, total, (ps, pr, cs, cr))
-    next_out[...] = total[...].astype(jnp.bfloat16)
+        part[:, :, here] = piece.reshape(count // 2, held, tile)
+
+    (total,) = reduce_chunks(count, [field_of(part, scratch)], added, half_chunk)
+    half = total.shape[1]
+    core = me % 2
+    first, second = total[:wanted], total[wanted : 2 * wanted]
+    filler = [jnp.zeros((next_out.shape[0] - wanted, half), jnp.float32)]
+    keep = jnp.concatenate([jnp.where(core == 0, first, second)] + filler, axis=0)
+    give = jnp.concatenate([jnp.where(core == 0, second, first)] + filler, axis=0)
+    swap_out[...] = give.astype(jnp.bfloat16)
+    swap = remote(
+        swap_out, swap_in, swap_sem.at[0], swap_sem.at[1], "groups", sibling_of(me)
+    )
+    swap.start()
+    next_out[:, pl.ds(pl.multiple_of(core * half, HD), half)] = keep.astype(jnp.bfloat16)
+    swap.wait_recv()
+    next_out[:, pl.ds(pl.multiple_of((1 - core) * half, HD), half)] = swap_in[...]
+    swap.wait_send()
 
     @pl.loop(1, splits)
     def _(k):
@@ -595,7 +592,9 @@
         ),
         in_specs=[VMEM] * 4,
         out_specs=(VMEM, VMEM),
-        scratch_shapes=reduce_scratch(count, chunk, wide) + gather_sems(count),
+        scratch_shapes=[pltpu.VMEM((count, chunk, wide), jnp.float32)]
+        + reduce_scratch(count, chunk, wide, jnp.bfloat16)
+        + gather_sems(count),
         compiler_params=pltpu.CompilerParams(
             collective_id=0, has_side_effects=True, vmem_limit_bytes=LIMIT
         ),
@@ -659,23 +658,13 @@
         listed[:, None],
     )
 
-    chips = count // 2
     heads_out = pl.pallas_call(
         functools.partial(combine_kernel, count),
         out_shape=jax.ShapeDtypeStruct((count, chunk, depth), jnp.bfloat16),
         in_specs=[VMEM] * 2,
         out_specs=VMEM,
-        scratch_shapes=[
-            pltpu.VMEM((chips, chunk, depth), jnp.float32),
-            pltpu.VMEM((chips, chunk, HD), jnp.float32),
-            pltpu.VMEM((chips, chunk, depth), jnp.bfloat16),
-            pltpu.VMEM((chips, chunk, HD), jnp.float32),
-            pltpu.VMEM((chips, chunk, depth), jnp.bfloat16),
-            pltpu.VMEM((chips, chunk, HD), jnp.float32),
-            pltpu.VMEM((chunk, depth), jnp.float32),
-            pltpu.VMEM((chunk, HD), jnp.float32),
-        ]
-        + [pltpu.SemaphoreType.DMA((chips,))] * 8
+        scratch_shapes=reduce_scratch(count, chunk, depth, jnp.bfloat16)
+        + reduce_scratch(count, chunk, HD, jnp.float32)
         + gather_sems(count),
         compiler_params=pltpu.CompilerParams(
             collective_id=1, has_side_effects=True, vmem_limit_bytes=LIMIT
@@ -683,13 +672,15 @@
         name="combine",
     )(numer.reshape(count, chunk, depth), stats.reshape(count, chunk, HD))
 
-    held = round_up(row_count // count, 16)
+    share = row_count // count
+    held = round_up(2 * share, 8)
+    given = round_up(share, 16)
     next_wide = next_weight.shape[1]
     hidden_out, next_out = pl.pallas_call(
-        functools.partial(output_kernel, count, splits, row_count // count),
+        functools.partial(output_kernel, count, splits, share),
         out_shape=(
             jax.ShapeDtypeStruct((height, model_part), jnp.bfloat16),
-            jax.ShapeDtypeStruct((held, next_wide), jnp.bfloat16),
+            jax.ShapeDtypeStruct((given, next_wide), jnp.bfloat16),
         ),
         in_specs=[VMEM, VMEM, VMEM, ANY, ANY],
         out_specs=(VMEM, VMEM),
@@ -704,9 +695,13 @@
             pltpu.SemaphoreType.DMA((count,)),
             pltpu.SemaphoreType.DMA((count,)),
             pltpu.VMEM((height, model_part), jnp.float32),
-            pltpu.VMEM((count, held, model_part), jnp.float32),
+            pltpu.VMEM((count // 2, held, model_part), jnp.float32),
+            pltpu.VMEM((given, next_wide // 2), jnp.bfloat16),
+            pltpu.VMEM((given, next_wide // 2), jnp.bfloat16),
+            pltpu.SemaphoreType.DMA((2,)),
+            pltpu.VMEM((count // 2, held, next_wide), jnp.float32),
         ]
-        + reduce_scratch(count, held, next_wide),
+        + reduce_scratch(count, held, next_wide // 2, jnp.float32),
         compiler_params=pltpu.CompilerParams(
             collective_id=2, has_side_effects=True, vmem_limit_bytes=LIMIT
         ),
@@ -715,7 +710,7 @@
     if chunk != own:
         hidden_out = hidden_out.reshape(blocks, chunk, model_part)[:, :own]
         hidden_out = hidden_out.reshape(row_count, model_part)
-    return (hidden_out, next_out[: row_count // count])
+    return (hidden_out, next_out[:share])
 
 
 def solution(mesh):

time: 193 us -> 175 us (0.907); the launches traced: 193 us -> 173 us
  Pallas kernels: 180 us -> 160 us
    pallas_call x1, Pallas kernels: 51.9 us -> 42.2 us  [on_device(): pl.pallas_call(functools.partial(combine_kernel, count), out_shape=jax.Sh...]
    pallas_call x1, Pallas kernels: 54.1 us -> 47 us  [on_device(): pl.pallas_call(functools.partial(project_kernel, count), out_shape=(jax.S...]
    pallas_call x1, Pallas kernels: 59.6 us -> 56 us  [on_device(): pl.pallas_call(functools.partial(output_kernel, count, splits, share), ou...]
where the time goes in v2:
time: 175 us; the launch traced here: 173 us
  Pallas kernels  160 us (91%)
  other arithmetic  6.46 us (4%)
  local copies, waits for them, and re-layouts  5.43 us (3%)
    pallas_call x1, Pallas kernels, on_device(): pl.pallas_call(functools.partial(output_kernel, count, splits, share), ou...  56 us
    pallas_call x1, Pallas kernels, on_device(): pl.pallas_call(functools.partial(project_kernel, count), out_shape=(jax.S...  47 us
    pallas_call x1, Pallas kernels, on_device(): pl.pallas_call(functools.partial(combine_kernel, count), out_shape=jax.Sh...  42.2 us
    pallas_call x1, Pallas kernels, on_device(): pl.pallas_call(attend_kernel, grid=(kv_local,), out_shape=(jax.ShapeDtype...  14.7 us

profile of v2, /device:TPU:10, one launch (start us, length us, event | category | flops | bytes accessed | tf_op | source)
XLA Modules:
  0.0 172.5 jit_solution(18132753237505690149)
XLA Ops:
  0.7 0.7 fusion.5
  1.3 0.8 compare_select_fusion
  2.1 0.1 broadcast_select_fusion
  2.2 0.7 fusion.7
  2.9 0.1 pad.2.clone
  2.9 0.1 copy.16
  3.1 0.1 reduce
  3.2 0.7 fusion.8
  3.9 0.8 select_reduce_fusion
  4.7 0.1 add_bitcast_fusion
  4.8 0.8 compare_reduce_fusion
  5.6 0.1 fusion.3
  5.7 0.6 broadcast_in_dim.74.key_pos
  6.3 0.1 fusion.4
  6.4 0.7 pad_maximum_fusion.2
  7.1 0.2 fusion
  7.3 0.7 pad_maximum_fusion
  7.9 1.4 copy.17.listed
  9.4 47.0 %project.1 = (bf16[16,48,1024]{2,1,0:T(8,128)(2,1)}, bf16[48,256]{1,0:T(8,128)(2,1)}) custom-call(bf16[192,512]{1,0:T(8,128)(2,1)} %hidden.3, bf16[512,5120]{1,0:T(8,128)(2,1)} %weight.1, f32[48,128]{1,0:T(8,128)} %get-tuple-element.29.cosine, f32[48,128]{1,0:T(8,128)} %get-tuple-element.30.sine), custom_call_target="tpu_custom_call" | custom-call | tf_op jit(solution)/shard_map/project/pallas_call | solution.py:587
  56.4 14.7 %attend.1 = (f32[4,4,48,1024]{3,2,1,0:T(8,128)}, f32[4,4,48,128]{3,2,1,0:T(8,128)}) custom-call(bf16[4,4,48,1024]{3,2,1,0:T(8,128)(2,1)} %bitcast.17, bf16[768,512]{1,0:T(8,128)(2,1)} %cache_keys.1, bf16[768,512]{1,0:T(8,128)(2,1)} %cache_values.1, f32[6,128]{1,0:T(8,128)} %get-tuple-element.31.cosine, f32[6,128]{1,0:T(8,128)} %get-tuple-element.32.sine, ...), custom_call_target="tpu_custom_call" | custom-call | tf_op jit(solution)/shard_map/attend/pallas_call | solution.py:622
  71.1 42.2 %combine.1.heads_out = bf16[16,48,1024]{2,1,0:T(8,128)(2,1)} custom-call(f32[16,48,1024]{2,1,0:T(8,128)} %bitcast.16, f32[16,48,128]{2,1,0:T(8,128)} %bitcast.18), custom_call_target="tpu_custom_call" | custom-call | tf_op jit(solution)/shard_map/combine/pallas_call | solution.py:661
  113.3 56.0 %output.1 = (bf16[192,512]{1,0:T(8,128)(2,1)}, bf16[16,5120]{1,0:T(8,128)(2,1)}) custom-call(bf16[16,48,1024]{2,1,0:T(8,128)(2,1)} %combine.1.heads_out, bf16[192,512]{1,0:T(8,128)(2,1)} %hidden.3, f32[1,512]{1,0:T(1,128)} %bitcast.21, bf16[4096,512]{1,0:T(8,128)(2,1)} %out_weight.1, bf16[512,5120]{1,0:T(8,128)(2,1)} %next_weight.1), custom_call_target="tpu_custom_call" | custom-call | tf_op jit(solution)/shard_map/output/pallas_call | solution.py:679
  169.3 1.6 copy.20
  170.9 1.6 copy.21
  (8 shorter events, 0.1 us)
